TPU v7x, 32 devices: a whole 2x2x4 slice. The times are simulated.
32 devices in a mesh: bunch: 16 (over z, x, core), dom: 2 (over y).
Axes of the slice: x: 2, y: 2, z: 4, core: 2. Of those that a mesh axis runs over, the one named last changes fastest.
Arguments:
- coords: float32 [4, 128, 65536], P(None, 'bunch', 'dom'), may hold values from -6 to 6
- slice_index: int32 [128, 65536], P('bunch', 'dom'), may hold values from 0 to 511
- fill: int32 [1792], P('bunch'), may hold values 0 or 1
- untracked_slot_centres: float32 [2, 1792], P(None, 'bunch'), may hold values from -0.046875 to 0.046875
- wake: float32 [4, 512, 64], replicated, may hold values from -0.75 to 0.75
- term_decay_factor: float32 [2, 8], replicated, may hold values from 0 to 1, as said below
- lr_coef: float32 [2, 8], replicated, may hold values from 0.5 to 5
- tunes: float32 [2], replicated, may hold values from 0.26 to 0.32
- chroma: float32 [2], replicated, may hold values from -3 to 3
Outputs:
- coords_out: float32 [4, 128, 65536], P(None, 'bunch', 'dom')
Inputs may be any that keep to these rules, and one draw needn't show every extreme that they name: `term_decay_factor`: rates of at least 0.1 / 1792.
All inputs are finite; a program needn't handle non-finite values. No bound on the sum of `fill` on one device may be relied on, other than what follows from the above.
Results may differ from a plain program's by a relative error of at most 0.0002.
Values sent between devices are 32-bit elements; how exact they have to be, the bound alone decides.
A program may use at most 128 MiB of HBM per device.

v0:
```python
import math

import jax
import jax.numpy as jnp
from jax import lax
from jax.sharding import PartitionSpec as P

SLICES = 512
BAND = 64


def from_behind(value, axis, steps):
    count = lax.axis_size(axis)
    pairs = [(source, (source + steps) % count) for source in range(count)]
    return lax.ppermute(value, axis, pairs)


def slice_tables(wake):
    four, slices, band = wake.shape
    blocks = slices // band
    shaped = wake.reshape(four, blocks, band, band)
    row_ids = jnp.arange(band)[:, None]
    col_ids = jnp.arange(band)[None, :]
    offset = (col_ids - row_ids) % band
    table = shaped[:, :, jnp.broadcast_to(col_ids, (band, band)), offset]
    lower = col_ids >= row_ids
    return (jnp.where(lower, table, 0.0), jnp.where(lower, 0.0, table))


def reorder(moments):
    return jnp.stack([moments[:, 1], moments[:, 0], moments[:, 2], moments[:, 0]], axis=1)


def block_kicks(blocked, previous, diag_table, off_table):
    near = jnp.einsum(
        "bcqj,cqjk->bcqk",
        blocked,
        diag_table,
        precision=lax.Precision.HIGHEST,
        preferred_element_type=jnp.float32,
    )
    far = jnp.einsum(
        "bcqj,cqjk->bcqk",
        previous,
        off_table,
        precision=lax.Precision.HIGHEST,
        preferred_element_type=jnp.float32,
    )
    return near + far


def on_device(
    coords,
    slice_index,
    fill,
    untracked_slot_centres,
    wake,
    term_decay_factor,
    lr_coef,
    tunes,
    chroma,
):
    bunch_dev = coords.shape[1]
    part_dev = coords.shape[2]
    slot_dev = fill.shape[0]
    n_dom = lax.axis_size("dom")
    n_cycle = lax.axis_size("bunch")
    scale_moment = SLICES / (part_dev * n_dom)
    block_len = min(part_dev, 4096)
    block_count = part_dev // block_len
    level_values = jnp.arange(SLICES, dtype=jnp.int32)

    def deposit_block(step, total):
        start = step * block_len
        index_piece = lax.dynamic_slice_in_dim(slice_index, start, block_len, 1)
        pos_piece = lax.dynamic_slice_in_dim(coords[0], start, block_len, 1)
        posy_piece = lax.dynamic_slice_in_dim(coords[2], start, block_len, 1)
        onehot = (index_piece[:, :, None] == level_values[None, None, :]).astype(jnp.float32)
        values = jnp.stack([jnp.ones_like(pos_piece), pos_piece, posy_piece], axis=1)
        return total + jnp.einsum(
            "bvp,bps->bvs",
            values,
            onehot,
            precision=lax.Precision.HIGHEST,
            preferred_element_type=jnp.float32,
        )

    partial_value = lax.fori_loop(
        0, block_count, deposit_block, jnp.zeros((bunch_dev, 3, SLICES), jnp.float32)
    )
    diag_table, off_table = slice_tables(wake)
    moments = lax.psum(partial_value, "dom") * scale_moment
    source = reorder(moments)
    blocks = SLICES // BAND
    blocked = source.reshape(bunch_dev, 4, blocks, BAND)
    previous = jnp.concatenate([jnp.zeros_like(blocked[:, :, :1]), blocked[:, :, :-1]], axis=2)
    slice_kick = block_kicks(blocked, previous, diag_table, off_table).reshape(bunch_dev, 4, SLICES)
    centre_sum = jnp.sum(moments[:, 1:3], axis=2)
    tracked = centre_sum / SLICES
    combined_result = jnp.concatenate(
        [tracked, jnp.transpose(untracked_slot_centres)[bunch_dev:]], axis=0
    )
    bunch_centre = fill.astype(jnp.float32)[:, None] * combined_result
    slot_float = jnp.arange(slot_dev, dtype=jnp.float32)
    tail_weight = jnp.exp(-term_decay_factor[None] * (slot_dev - 1 - slot_float)[:, None, None])
    block_sum = jnp.sum(tail_weight * bunch_centre[:, :, None], axis=0)
    track_float = jnp.arange(bunch_dev, dtype=jnp.float32)
    spacing = track_float[:, None] - slot_float[None, :] - 1.0
    earlier_mask = spacing >= 0.0
    inner = jnp.where(
        earlier_mask[None, None],
        jnp.exp(
            -term_decay_factor[:, :, None, None] * jnp.where(earlier_mask, spacing, 0.0)[None, None]
        ),
        0.0,
    )
    in_block = jnp.einsum(
        "crij,jc->icr",
        inner,
        bunch_centre,
        precision=lax.Precision.HIGHEST,
        preferred_element_type=jnp.float32,
    )
    block_decay = jnp.exp(-term_decay_factor * slot_dev)

    def pass_once(turn, carried):
        return from_behind(block_decay * carried + block_sum, "bunch", 1)

    carried = lax.fori_loop(0, n_cycle - 1, pass_once, jnp.zeros_like(block_sum))
    incoming = carried + jnp.exp(-term_decay_factor * slot_dev * (n_cycle - 1)) * block_sum
    incoming = incoming / (1.0 - jnp.exp(-term_decay_factor * (slot_dev * n_cycle)))
    state = (
        jnp.exp(-term_decay_factor[None] * track_float[:, None, None]) * incoming[None] + in_block
    )
    long_kick = jnp.sum(state * lr_coef[None], axis=2)

    def track_block(step, result):
        start = step * block_len
        piece = lax.dynamic_slice_in_dim(coords, start, block_len, 2)
        index_piece = lax.dynamic_slice_in_dim(slice_index, start, block_len, 1)
        onehot = (index_piece[:, :, None] == level_values[None, None, :]).astype(jnp.float32)
        kicks = jnp.einsum(
            "bcs,bps->bcp",
            slice_kick,
            onehot,
            precision=lax.Precision.HIGHEST,
            preferred_element_type=jnp.float32,
        )
        pos_x, mom_x, pos_y, mom_y = (piece[0], piece[1], piece[2], piece[3])
        mom_xk = mom_x + kicks[:, 0] + kicks[:, 1] * pos_x + long_kick[:, 0:1]
        mom_yk = mom_y + kicks[:, 2] + kicks[:, 3] * pos_y + long_kick[:, 1:2]
        slice_pos = 2.0 * (index_piece.astype(jnp.float32) + 0.5) / SLICES - 1.0
        phase_x = 2.0 * math.pi * tunes[0] + chroma[0] * slice_pos
        phase_y = 2.0 * math.pi * tunes[1] + chroma[1] * slice_pos
        cos_x, sin_x = (jnp.cos(phase_x), jnp.sin(phase_x))
        cos_y, sin_y = (jnp.cos(phase_y), jnp.sin(phase_y))
        turned = jnp.stack(
            [
                cos_x * pos_x + sin_x * mom_xk,
                cos_x * mom_xk - sin_x * pos_x,
                cos_y * pos_y + sin_y * mom_yk,
                cos_y * mom_yk - sin_y * pos_y,
            ],
            axis=0,
        )
        return lax.dynamic_update_slice_in_dim(result, turned, start, 2)

    return lax.fori_loop(0, block_count, track_block, jnp.zeros_like(coords))


def solution(mesh):
    placed = (
        P(None, "bunch", "dom"),
        P("bunch", "dom"),
        P("bunch"),
        P(None, "bunch"),
        P(),
        P(),
        P(),
        P(),
        P(),
    )
    return jax.shard_map(
        on_device, mesh=mesh, in_specs=placed, out_specs=P(None, "bunch", "dom"), check_vma=False
    )
```

profile of v0, /device:TPU:0, one launch (start us, length us, event | category | flops | bytes accessed | tf_op | source)
XLA Modules:
  0.0 734.3 jit_solution(4287973949792572668)
XLA Ops:
  0.0 7.0 copy.59
  7.0 216.0 %while.42 = (s32[]{:T(128)}, f32[8,3,512]{2,1,0:T(4,128)S(1)}, f32[4,8,32768]{2,0,1:T(4,128)}, s32[8,32768]{1,0:T(8,128)S(1)}, s32[]{:T(128)}, /*index=5*/s32[]{:T(128)}, s32[]{:T(128)}, s32[]{:T(128)}, f32[]{:T(128)}, f32[]{:T(128)}) while((s32[]{:T(128)}, f32[8,3,512]{2,1,0:T(4,128)S(1)}, f32[4,8,32768]{2,0,1:T(4,128)}, ...), condition=%wide.region_1.0_spmd.clone, body=%wide.region_0.0_spmd.clone.sunk | while | flops 620978176 | bytes 5472453 | solution.py:88
  7.0 5.6 fusion.82
  12.6 21.4 %fusion.83 = f32[8,3,512]{2,1,0:T(4,128)S(1)} fusion(s32[8,4096]{1,0:T(8,128)S(1)} %constant_dynamic-slice_fusion.5, f32[8,1,4096]{2,1,0:T(1,128)S(1)} %get-tuple-element.640, f32[8,1,4096]{2,1,0:T(1,128)S(1)} %get-tuple-element.641, f32[3]{0:T(128)S(1)} %pad.5.clone.2, f32[8,3,512]{2,1,0:T(4,128)S(1)} %get-tuple-element.653, pred[]{:T(512)S(6)} %compare.11), kind=kOutput, calls=%fused_computation.41.clone.1 | convolution fusion | flops 620978176 | bytes 491533 | tf_op jit(solution)/shard_map/while/body/eval_jaxpr/bvp,bps->bvs/dot_general | solution.py:80
  34.0 5.5 fusion.82
  39.6 21.4 %fusion.83 = f32[8,3,512]{2,1,0:T(4,128)S(1)} fusion(s32[8,4096]{1,0:T(8,128)S(1)} %constant_dynamic-slice_fusion.5, f32[8,1,4096]{2,1,0:T(1,128)S(1)} %get-tuple-element.640, f32[8,1,4096]{2,1,0:T(1,128)S(1)} %get-tuple-element.641, f32[3]{0:T(128)S(1)} %pad.5.clone.2, f32[8,3,512]{2,1,0:T(4,128)S(1)} %get-tuple-element.653, pred[]{:T(512)S(6)} %compare.11), kind=kOutput, calls=%fused_computation.41.clone.1 | convolution fusion | flops 620978176 | bytes 491533 | tf_op jit(solution)/shard_map/while/body/eval_jaxpr/bvp,bps->bvs/dot_general | solution.py:80
  61.0 5.5 fusion.82
  66.6 21.4 %fusion.83 = f32[8,3,512]{2,1,0:T(4,128)S(1)} fusion(s32[8,4096]{1,0:T(8,128)S(1)} %constant_dynamic-slice_fusion.5, f32[8,1,4096]{2,1,0:T(1,128)S(1)} %get-tuple-element.640, f32[8,1,4096]{2,1,0:T(1,128)S(1)} %get-tuple-element.641, f32[3]{0:T(128)S(1)} %pad.5.clone.2, f32[8,3,512]{2,1,0:T(4,128)S(1)} %get-tuple-element.653, pred[]{:T(512)S(6)} %compare.11), kind=kOutput, calls=%fused_computation.41.clone.1 | convolution fusion | flops 620978176 | bytes 491533 | tf_op jit(solution)/shard_map/while/body/eval_jaxpr/bvp,bps->bvs/dot_general | solution.py:80
  88.0 5.5 fusion.82
  93.6 21.4 %fusion.83 = f32[8,3,512]{2,1,0:T(4,128)S(1)} fusion(s32[8,4096]{1,0:T(8,128)S(1)} %constant_dynamic-slice_fusion.5, f32[8,1,4096]{2,1,0:T(1,128)S(1)} %get-tuple-element.640, f32[8,1,4096]{2,1,0:T(1,128)S(1)} %get-tuple-element.641, f32[3]{0:T(128)S(1)} %pad.5.clone.2, f32[8,3,512]{2,1,0:T(4,128)S(1)} %get-tuple-element.653, pred[]{:T(512)S(6)} %compare.11), kind=kOutput, calls=%fused_computation.41.clone.1 | convolution fusion | flops 620978176 | bytes 491533 | tf_op jit(solution)/shard_map/while/body/eval_jaxpr/bvp,bps->bvs/dot_general | solution.py:80
  115.0 5.5 fusion.82
  120.6 21.4 %fusion.83 = f32[8,3,512]{2,1,0:T(4,128)S(1)} fusion(s32[8,4096]{1,0:T(8,128)S(1)} %constant_dynamic-slice_fusion.5, f32[8,1,4096]{2,1,0:T(1,128)S(1)} %get-tuple-element.640, f32[8,1,4096]{2,1,0:T(1,128)S(1)} %get-tuple-element.641, f32[3]{0:T(128)S(1)} %pad.5.clone.2, f32[8,3,512]{2,1,0:T(4,128)S(1)} %get-tuple-element.653, pred[]{:T(512)S(6)} %compare.11), kind=kOutput, calls=%fused_computation.41.clone.1 | convolution fusion | flops 620978176 | bytes 491533 | tf_op jit(solution)/shard_map/while/body/eval_jaxpr/bvp,bps->bvs/dot_general | solution.py:80
  142.0 5.5 fusion.82
  147.6 21.4 %fusion.83 = f32[8,3,512]{2,1,0:T(4,128)S(1)} fusion(s32[8,4096]{1,0:T(8,128)S(1)} %constant_dynamic-slice_fusion.5, f32[8,1,4096]{2,1,0:T(1,128)S(1)} %get-tuple-element.640, f32[8,1,4096]{2,1,0:T(1,128)S(1)} %get-tuple-element.641, f32[3]{0:T(128)S(1)} %pad.5.clone.2, f32[8,3,512]{2,1,0:T(4,128)S(1)} %get-tuple-element.653, pred[]{:T(512)S(6)} %compare.11), kind=kOutput, calls=%fused_computation.41.clone.1 | convolution fusion | flops 620978176 | bytes 491533 | tf_op jit(solution)/shard_map/while/body/eval_jaxpr/bvp,bps->bvs/dot_general | solution.py:80
  169.0 5.5 fusion.82
  174.6 21.4 %fusion.83 = f32[8,3,512]{2,1,0:T(4,128)S(1)} fusion(s32[8,4096]{1,0:T(8,128)S(1)} %constant_dynamic-slice_fusion.5, f32[8,1,4096]{2,1,0:T(1,128)S(1)} %get-tuple-element.640, f32[8,1,4096]{2,1,0:T(1,128)S(1)} %get-tuple-element.641, f32[3]{0:T(128)S(1)} %pad.5.clone.2, f32[8,3,512]{2,1,0:T(4,128)S(1)} %get-tuple-element.653, pred[]{:T(512)S(6)} %compare.11), kind=kOutput, calls=%fused_computation.41.clone.1 | convolution fusion | flops 620978176 | bytes 491533 | tf_op jit(solution)/shard_map/while/body/eval_jaxpr/bvp,bps->bvs/dot_general | solution.py:80
  196.0 5.5 fusion.82
  201.6 21.4 %fusion.83 = f32[8,3,512]{2,1,0:T(4,128)S(1)} fusion(s32[8,4096]{1,0:T(8,128)S(1)} %constant_dynamic-slice_fusion.5, f32[8,1,4096]{2,1,0:T(1,128)S(1)} %get-tuple-element.640, f32[8,1,4096]{2,1,0:T(1,128)S(1)} %get-tuple-element.641, f32[3]{0:T(128)S(1)} %pad.5.clone.2, f32[8,3,512]{2,1,0:T(4,128)S(1)} %get-tuple-element.653, pred[]{:T(512)S(6)} %compare.11), kind=kOutput, calls=%fused_computation.41.clone.1 | convolution fusion | flops 620978176 | bytes 491533 | tf_op jit(solution)/shard_map/while/body/eval_jaxpr/bvp,bps->bvs/dot_general | solution.py:80
  223.0 10.6 %psum.7 = f32[8,3,512]{2,1,0:T(4,128)S(1)} all-reduce(f32[8,3,512]{2,1,0:T(4,128)S(1)} %get-tuple-element.349), channel_id=1, replica_groups=mesh['bunch'=16,'dom'=2] {'dom'}, use_global_device_ids=true, to_apply=%region_2.3 | all-reduce | flops 12288 | bytes 98304 | tf_op jit(solution)/shard_map/psum | solution.py:92
  234.1 5.4 copy.57
  239.6 40.4 %gather_fusion = f32[4096,4,8]{2,1,0:T(4,128)} fusion(f32[4,8,64,64]{1,0,3,2:T(4,128)} %copy.57, s32[4096]{0:T(1024)S(1)} %reshape.155), kind=kCustom, calls=%fused_computation | custom fusion | bytes 1081344 | tf_op jit(solution)/shard_map/gather | solution.py:25
  280.0 6.8 copy.58
  289.7 85.5 %while.40 = (s32[]{:T(128)}, f32[2,8]{1,0:T(2,128)S(1)}, f32[2,8]{1,0:T(2,128)S(1)}, f32[2,8]{1,0:T(2,128)S(1)}, s32[]{:T(128)}) while((s32[]{:T(128)}, f32[2,8]{1,0:T(2,128)S(1)}, f32[2,8]{1,0:T(2,128)S(1)}, f32[2,8]{1,0:T(2,128)S(1)}, s32[]{:T(128)}) %tuple.119), condition=%wide.region_6.7_spmd, body=%wide.region_5.6_spmd.sunk | while | flops 34 | bytes 613 | solution.py:129
  289.8 5.7 collective-permute-done
  295.5 5.7 collective-permute-done
  301.2 5.7 collective-permute-done
  306.9 5.7 collective-permute-done
  312.6 5.7 collective-permute-done
  318.3 5.7 collective-permute-done
  324.0 5.7 collective-permute-done
  329.6 5.7 collective-permute-done
  335.3 5.7 collective-permute-done
  341.0 5.7 collective-permute-done
  346.7 5.7 collective-permute-done
  352.4 5.7 collective-permute-done
  358.1 5.7 collective-permute-done
  363.8 5.7 collective-permute-done
  369.5 5.7 collective-permute-done
  380.6 353.7 %while.41 = (s32[]{:T(128)}, f32[4,8,32768]{2,1,0:T(8,128)}, f32[]{:T(128)}, f32[2]{0:T(128)S(1)}, s32[8,32768]{1,0:T(8,128)S(1)}, /*index=5*/f32[4,8,32768]{2,1...) while((s32[]{:T(128)}, f32[4,8,32768]{2,1,0:T(8,128)}, ...), condition=%wide.region_9.10_spmd.clone, body=%wide.region_8.9_spmd.clone.sunk | while | flops 823787520 | bytes 5833211 | solution.py:168
  380.7 34.9 %fusion.79 = f32[8,4,4096]{2,1,0:T(4,128)S(1)} fusion(f32[8,4,512]{2,1,0:T(4,128)S(1)} %get-tuple-element.725, s32[8,4096]{1,0:T(8,128)S(1)} %constant_dynamic-slice_fusion.4), kind=kOutput, calls=%fused_computation.7.clone.1 | convolution fusion | flops 822083584 | bytes 720896 | tf_op jit(solution)/shard_map/while/body/eval_jaxpr/bcs,bps->bcp/dot_general | solution.py:142
  418.8 3.2 add_bitcast_fusion.5
  424.9 34.9 %fusion.79 = f32[8,4,4096]{2,1,0:T(4,128)S(1)} fusion(f32[8,4,512]{2,1,0:T(4,128)S(1)} %get-tuple-element.725, s32[8,4096]{1,0:T(8,128)S(1)} %constant_dynamic-slice_fusion.4), kind=kOutput, calls=%fused_computation.7.clone.1 | convolution fusion | flops 822083584 | bytes 720896 | tf_op jit(solution)/shard_map/while/body/eval_jaxpr/bcs,bps->bcp/dot_general | solution.py:142
  469.1 34.9 %fusion.79 = f32[8,4,4096]{2,1,0:T(4,128)S(1)} fusion(f32[8,4,512]{2,1,0:T(4,128)S(1)} %get-tuple-element.725, s32[8,4096]{1,0:T(8,128)S(1)} %constant_dynamic-slice_fusion.4), kind=kOutput, calls=%fused_computation.7.clone.1 | convolution fusion | flops 822083584 | bytes 720896 | tf_op jit(solution)/shard_map/while/body/eval_jaxpr/bcs,bps->bcp/dot_general | solution.py:142
  513.3 34.9 %fusion.79 = f32[8,4,4096]{2,1,0:T(4,128)S(1)} fusion(f32[8,4,512]{2,1,0:T(4,128)S(1)} %get-tuple-element.725, s32[8,4096]{1,0:T(8,128)S(1)} %constant_dynamic-slice_fusion.4), kind=kOutput, calls=%fused_computation.7.clone.1 | convolution fusion | flops 822083584 | bytes 720896 | tf_op jit(solution)/shard_map/while/body/eval_jaxpr/bcs,bps->bcp/dot_general | solution.py:142
  557.5 34.9 %fusion.79 = f32[8,4,4096]{2,1,0:T(4,128)S(1)} fusion(f32[8,4,512]{2,1,0:T(4,128)S(1)} %get-tuple-element.725, s32[8,4096]{1,0:T(8,128)S(1)} %constant_dynamic-slice_fusion.4), kind=kOutput, calls=%fused_computation.7.clone.1 | convolution fusion | flops 822083584 | bytes 720896 | tf_op jit(solution)/shard_map/while/body/eval_jaxpr/bcs,bps->bcp/dot_general | solution.py:142
  601.7 34.9 %fusion.79 = f32[8,4,4096]{2,1,0:T(4,128)S(1)} fusion(f32[8,4,512]{2,1,0:T(4,128)S(1)} %get-tuple-element.725, s32[8,4096]{1,0:T(8,128)S(1)} %constant_dynamic-slice_fusion.4), kind=kOutput, calls=%fused_computation.7.clone.1 | convolution fusion | flops 822083584 | bytes 720896 | tf_op jit(solution)/shard_map/while/body/eval_jaxpr/bcs,bps->bcp/dot_general | solution.py:142
  645.9 34.9 %fusion.79 = f32[8,4,4096]{2,1,0:T(4,128)S(1)} fusion(f32[8,4,512]{2,1,0:T(4,128)S(1)} %get-tuple-element.725, s32[8,4096]{1,0:T(8,128)S(1)} %constant_dynamic-slice_fusion.4), kind=kOutput, calls=%fused_computation.7.clone.1 | convolution fusion | flops 822083584 | bytes 720896 | tf_op jit(solution)/shard_map/while/body/eval_jaxpr/bcs,bps->bcp/dot_general | solution.py:142
  690.1 34.9 %fusion.79 = f32[8,4,4096]{2,1,0:T(4,128)S(1)} fusion(f32[8,4,512]{2,1,0:T(4,128)S(1)} %get-tuple-element.725, s32[8,4096]{1,0:T(8,128)S(1)} %constant_dynamic-slice_fusion.4), kind=kOutput, calls=%fused_computation.7.clone.1 | convolution fusion | flops 822083584 | bytes 720896 | tf_op jit(solution)/shard_map/while/body/eval_jaxpr/bcs,bps->bcp/dot_general | solution.py:142
  (165 shorter events, 79.2 us)
Async XLA Ops:
  0.0 7.0 copy-start
  7.0 226.9 %copy-start.1 = (f32[4,512,64]{1,2,0:T(8,128)S(1)}, f32[4,512,64]{1,2,0:T(8,128)}, u32[]{:S(2)}) copy-start(f32[4,512,64]{1,2,0:T(8,128)} %param.19) | copy-start | bytes 1572868
  279.9 9.2 %copy-start.3 = (f32[2,8]{1,0:T(2,128)S(1)}, f32[2,8]{1,0:T(2,128)}, u32[]{:S(2)}) copy-start(f32[2,8]{1,0:T(2,128)} %param.20) | copy-start | bytes 196
  279.9 9.4 %copy-start.6 = (f32[2,112]{1,0:T(2,128)S(1)}, f32[2,112]{1,0:T(2,128)}, u32[]{:S(2)}) copy-start(f32[2,112]{1,0:T(2,128)} %param.18) | copy-start | bytes 2692
  279.9 9.5 %copy-start.7 = (s32[112]{0:T(128)S(1)}, s32[112]{0:T(128)}, u32[]{:S(2)}) copy-start(s32[112]{0:T(128)} %param.17) | copy-start | bytes 1348
  279.9 96.4 %copy-start.5 = (f32[2,8]{1,0:T(2,128)S(1)}, f32[2,8]{1,0:T(2,128)}, u32[]{:S(2)}) copy-start(f32[2,8]{1,0:T(2,128)} %param.21) | copy-start | bytes 196
  279.9 96.5 %copy-start.4 = (f32[2]{0:T(128)S(1)}, f32[2]{0:T(128)}, u32[]{:S(2)}) copy-start(f32[2]{0:T(128)} %param.22) | copy-start | bytes 28
  286.8 93.8 %copy-start.2 = (f32[2]{0:T(128)S(1)}, f32[2]{0:T(128)}, u32[]{:S(2)}) copy-start(f32[2]{0:T(128)} %param.23) | copy-start | bytes 28
  289.7 5.7 collective-permute-start
  295.5 5.7 collective-permute-start
  301.2 5.7 collective-permute-start
  306.9 5.7 collective-permute-start
  312.6 5.7 collective-permute-start
  318.3 5.7 collective-permute-start
  323.9 5.7 collective-permute-start
  329.6 5.7 collective-permute-start
  335.3 5.7 collective-permute-start
  341.0 5.7 collective-permute-start
  346.7 5.7 collective-permute-start
  352.4 5.7 collective-permute-start
  358.1 5.7 collective-permute-start
  363.8 5.7 collective-permute-start
  369.5 5.7 collective-permute-start
where the time goes:
time: 736 us; the launch traced here: 734 us
  matrix products  453 us (62%)
  local copies, waits for them, and re-layouts  116 us (16%)
  waiting for transfers between devices  85.3 us (12%)
  other arithmetic  66.6 us (9%)
  blocking collectives  10.6 us (1%)
    dot_general x8, matrix products, track_block(): jnp.einsum('bcs,bps->bcp', slice_kick, onehot, precision=lax.Precision.HI...  279 us
    dot_general x8, matrix products, deposit_block(): jnp.einsum('bvp,bps->bvs', values, onehot, precision=lax.Precision.HIGHES...  171 us
    ppermute x15, waiting for transfers between devices, from_behind(): return lax.ppermute(value, axis, pairs)  85.3 us
    another operation x24, other arithmetic, track_block(): jnp.stack([cos_x * pos_x + sin_x * mom_xk, cos_x * mom_xk - sin_x * pos_x...  59.1 us
    gather x2, local copies, waits for them, and re-layouts, slice_tables(): table = shaped[:, :, jnp.broadcast_to(col_ids, (band, band)), offset]  47.2 us
    slice x8, local copies, waits for them, and re-layouts, deposit_block(): pos_piece = lax.dynamic_slice_in_dim(coords[0], start, block_len, 1)  44.2 us
  transfers between devices with their start and end apart: 15, of which 15 were waited for; matrix products, arithmetic and copies ran while one was open for 0% of the time, Pallas kernels for 0%

commit v1 on v0

v1 whole, which is shorter than its diff:
```python
import functools
import math

import jax
import jax.numpy as jnp
from jax import lax
from jax.experimental import pallas as pl
from jax.experimental.pallas import tpu as pltpu
from jax.sharding import PartitionSpec as P

SLICES = 512
BAND = 64
LANES = 128
PIECES = SLICES // LANES
LOW = 64
HIGH = SLICES // LOW
MESH = pl.DeviceIdType.MESH


def rows_sum(value):
    return jnp.sum(value, axis=0, keepdims=True)


def lanes_sum(value):
    return jnp.sum(value, axis=1, keepdims=True)


def deposit_kernel(
    n_cycle,
    n_dom,
    chunk,
    step_len,
    coords,
    index,
    fill,
    others,
    wake,
    decay,
    coef,
    tunes,
    chroma,
    tables,
    phases,
    x_buf,
    y_buf,
    i_buf,
    wake_t,
    grid_sum,
    slots,
    outgoing,
    block_own,
    block_got,
    mine,
    theirs,
    padded,
    in_sem,
    block_send,
    block_recv,
    dom_send,
    dom_recv,
):
    bunch_dev, part_dev = x_buf.shape
    slot_dev = fill.shape[1]
    chunks = part_dev // chunk
    me_b, me_d = lax.axis_index("bunch"), lax.axis_index("dom")

    def loads(step):
        where = pl.ds(pl.multiple_of(step * chunk, chunk), chunk)
        return (
            pltpu.make_async_copy(coords.at[0, :, where], x_buf.at[:, where], in_sem.at[0, step]),
            pltpu.make_async_copy(coords.at[2, :, where], y_buf.at[:, where], in_sem.at[1, step]),
            pltpu.make_async_copy(index.at[:, where], i_buf.at[:, where], in_sem.at[2, step]),
        )

    for plane in range(3):
        for step in range(chunks):
            loads(step)[plane].start()

    cycle_peers = [(lax.rem(me_b + k, n_cycle), me_d) for k in range(1, n_cycle)]
    dom_peers = [(me_b, lax.rem(me_d + k, n_dom)) for k in range(1, n_dom)]
    barrier = pltpu.get_barrier_semaphore()
    for peer in cycle_peers + dom_peers:
        pl.semaphore_signal(barrier, inc=1, device_id=peer, device_id_type=MESH)

    lane = lax.broadcasted_iota(jnp.int32, (8, LANES), 1)
    row = lax.broadcasted_iota(jnp.int32, (8, LANES), 0)
    second = lane >= 64
    half = jnp.where(second, lane - 64, lane)
    half_f = half.astype(jnp.float32)
    zeros = jnp.zeros((8, LANES), jnp.float32)

    def by_row(ref, plane):
        built = zeros
        for term in range(8):
            built = jnp.where(row == term, ref[plane, term], built)
        return built

    decay_x, decay_y = by_row(decay, 0), by_row(decay, 1)
    decay_both = jnp.where(second, decay_y, decay_x)
    coef_both = jnp.where(second, by_row(coef, 1), by_row(coef, 0))
    back = (slot_dev - 1 - lane).astype(jnp.float32)
    inside = lane < slot_dev
    back = jnp.where(inside, back, 0.0)
    tail_x = jnp.where(inside, jnp.exp(-decay_x * back), 0.0)
    tail_y = jnp.where(inside, jnp.exp(-decay_y * back), 0.0)
    block_decay = jnp.exp(-decay_both * slot_dev)
    closing = 1.0 - jnp.exp(-decay_both * (slot_dev * n_cycle))
    ahead = coef_both * jnp.exp(-decay_both * half_f)

    lower = row < 4
    chroma_rows = jnp.where(lower, chroma[0], chroma[1])
    tune_rows = jnp.where(lower, tunes[0], tunes[1])
    fine = chroma_rows * (lane.astype(jnp.float32) * (2.0 / SLICES))
    first = 2.0 * ((lane & 3).astype(jnp.float32) * LANES + 0.5) / SLICES - 1.0
    coarse = 2.0 * math.pi * tune_rows + chroma_rows * first
    fine_cos, fine_sin = jnp.cos(fine), jnp.sin(fine)
    coarse_cos, coarse_sin = jnp.cos(coarse), jnp.sin(coarse)
    for plane in range(2):
        at = 4 * plane
        base = plane * (2 + 2 * PIECES)
        phases[base] = jnp.broadcast_to(fine_cos[at : at + 1], (8, LANES))
        phases[base + 1] = jnp.broadcast_to(fine_sin[at : at + 1], (8, LANES))
        for piece in range(PIECES):
            spot = (slice(at, at + 1), slice(piece, piece + 1))
            phases[base + 2 + piece] = jnp.broadcast_to(coarse_cos[spot], (8, LANES))
            phases[base + 2 + PIECES + piece] = jnp.broadcast_to(coarse_sin[spot], (8, LANES))

    for plane in range(4):
        wake_t[plane] = jnp.transpose(wake[plane])
    slots[...] = jnp.zeros_like(slots)
    slots[0:2, 0:slot_dev] = others[...]
    slots[2:3, 0:slot_dev] = fill[...].astype(jnp.float32)

    def add_up(step, total):
        for plane in range(2):
            loads(step)[plane].wait()
        at = pl.multiple_of(step * chunk, chunk)
        sums = list(total)
        for piece in range(chunk // LANES):
            where = pl.ds(at + piece * LANES, LANES)
            k = piece % 4
            sums[k] = sums[k] + x_buf[:, where]
            sums[4 + k] = sums[4 + k] + y_buf[:, where]
        return tuple(sums)

    sums = lax.fori_loop(0, chunks, add_up, (zeros,) * 8)
    sum_x = lanes_sum((sums[0] + sums[1]) + (sums[2] + sums[3]))
    sum_y = lanes_sum((sums[4] + sums[5]) + (sums[6] + sums[7]))
    mean = 1.0 / (part_dev * n_dom)
    diagonal = lane == row
    once = jnp.where(me_d == 0, 1.0, 0.0)
    filled = slots[2:3, :]
    tracked = lane[0:1] < bunch_dev
    track_x = rows_sum(jnp.where(diagonal, sum_x, 0.0)) * mean
    track_y = rows_sum(jnp.where(diagonal, sum_y, 0.0)) * mean
    centre_x = filled * jnp.where(tracked, track_x, slots[0:1, :] * once)
    centre_y = filled * jnp.where(tracked, track_y, slots[1:2, :] * once)
    block_own[...] = jnp.where(
        second, lanes_sum(tail_y * centre_y), lanes_sum(tail_x * centre_x)
    )

    pl.semaphore_wait(barrier, n_cycle - 1 + n_dom - 1)

    def block_copy(k):
        return pltpu.make_async_remote_copy(
            src_ref=block_own,
            dst_ref=block_got.at[k],
            send_sem=block_send.at[k],
            recv_sem=block_recv.at[k],
            device_id=cycle_peers[k],
            device_id_type=MESH,
        )

    for k in range(n_cycle - 1):
        block_copy(k).start()

    grid_sum[...] = jnp.zeros_like(grid_sum)
    high_ids = lax.broadcasted_iota(jnp.int32, (HIGH, step_len), 0)
    low_ids = lax.broadcasted_iota(jnp.int32, (LOW, step_len), 0).astype(jnp.bfloat16)
    one, zero = jnp.bfloat16(1), jnp.bfloat16(0)
    shift = LOW.bit_length() - 1

    def deposit(step, _):
        at = pl.multiple_of(step * step_len, step_len)
        where = pl.ds(at, step_len)
        x, y, level = x_buf[:, where], y_buf[:, where], i_buf[:, where]
        x_low = x - x.astype(jnp.bfloat16).astype(jnp.float32)
        y_low = y - y.astype(jnp.bfloat16).astype(jnp.float32)
        high = lax.shift_right_logical(level, shift)
        low = (level & (LOW - 1)).astype(jnp.float32).astype(jnp.bfloat16)
        for b in range(bunch_dev):
            mask = high_ids == high[b : b + 1]
            values = (1.0, x[b : b + 1], y[b : b + 1], x_low[b : b + 1], y_low[b : b + 1])
            left = jnp.concatenate([jnp.where(mask, v, 0.0) for v in values], axis=0)
            right = jnp.where(low_ids == low[b : b + 1], one, zero)
            grid_sum[b] += lax.dot_general(
                left.astype(jnp.bfloat16),
                right,
                (((1,), (1,)), ((), ())),
                preferred_element_type=jnp.float32,
            )
        return 0

    for step in range(chunks):
        loads(step)[2].wait()
    lax.fori_loop(0, part_dev // step_len, deposit, 0)

    for b in range(bunch_dev):
        part = grid_sum[b]
        kinds = (
            part[0:HIGH],
            part[HIGH : 2 * HIGH] + part[3 * HIGH : 4 * HIGH],
            part[2 * HIGH : 3 * HIGH] + part[4 * HIGH : 5 * HIGH],
        )
        for v in range(3):
            for h in range(HIGH):
                at = v * SLICES + h * LOW
                mine[b : b + 1, at : at + LOW] = kinds[v][h : h + 1]

    carried = block_own[...]
    for k in reversed(range(n_cycle - 1)):
        block_copy(k).wait()
        carried = block_decay * carried + block_got[k]
    pieces = ahead * (carried / closing)
    for j in range(bunch_dev - 1):
        centre = jnp.where(second, centre_y[:, j : j + 1], centre_x[:, j : j + 1])
        gap = jnp.maximum(half - 1 - j, 0).astype(jnp.float32)
        inner = coef_both * jnp.exp(-decay_both * gap) * centre
        pieces = pieces + jnp.where(half > j, inner, 0.0)
    long_row = rows_sum(pieces)
    long_at = 3 * SLICES
    mine[:, long_at : long_at + LANES] = jnp.broadcast_to(
        lanes_sum(jnp.where(lane == row, long_row, 0.0)), (8, LANES)
    )
    mine[:, long_at + LANES : long_at + 2 * LANES] = jnp.broadcast_to(
        lanes_sum(jnp.where(lane == row + 64, long_row, 0.0)), (8, LANES)
    )

    def dom_copy(k):
        return pltpu.make_async_remote_copy(
            src_ref=mine,
            dst_ref=theirs.at[k],
            send_sem=dom_send.at[k],
            recv_sem=dom_recv.at[k],
            device_id=dom_peers[k],
            device_id_type=MESH,
        )

    for k in range(n_dom - 1):
        dom_copy(k).start()
    total = mine[...]
    for k in range(n_dom - 1):
        dom_copy(k).wait()
        total = total + theirs[k]

    scale_moment = SLICES / (part_dev * n_dom)
    for v in range(3):
        padded[v, :, 0:LANES] = zeros
        padded[v, :, LANES:] = total[:, v * SLICES : (v + 1) * SLICES] * scale_moment
    kicks = [jnp.zeros((8, SLICES), jnp.float32)] * 4
    for lag in range(BAND):
        count, mom_x, mom_y = (
            padded[v, :, LANES - lag : LANES - lag + SLICES] for v in range(3)
        )
        for c, source in enumerate((mom_x, count, mom_y, count)):
            kicks[c] = kicks[c] + wake_t[c, lag : lag + 1, :] * source
    long_x = total[:, long_at : long_at + 1]
    long_y = total[:, long_at + LANES : long_at + LANES + 1]
    tables[0] = kicks[0] + long_x
    tables[1] = kicks[1]
    tables[2] = kicks[2] + long_y
    tables[3] = kicks[3]


def track_kernel(
    chunk, unroll, coords, index, tables, phases, result, c_buf, i_buf, o_buf, in_sem, out_sem
):
    part_dev = i_buf.shape[1]
    chunks = part_dev // chunk

    def moves(step):
        where = pl.ds(step * chunk, chunk)
        return (
            pltpu.make_async_copy(
                coords.at[:, :, where], c_buf.at[:, :, where], in_sem.at[0, step]
            ),
            pltpu.make_async_copy(index.at[:, where], i_buf.at[:, where], in_sem.at[1, step]),
            pltpu.make_async_copy(
                o_buf.at[:, :, where], result.at[:, :, where], out_sem.at[step]
            ),
        )

    for step in range(chunks):
        load, load_index, _ = moves(step)
        load.start()
        load_index.start()

    def track(step, _):
        where = pl.ds(pl.multiple_of(step * LANES, LANES), LANES)
        level = i_buf[:, where]
        low = level & (LANES - 1)
        piece = lax.shift_right_logical(level, 7)
        odd, upper = (piece & 1) == 1, piece >= 2

        def pick(values):
            return jnp.where(
                upper,
                jnp.where(odd, values[3], values[2]),
                jnp.where(odd, values[1], values[0]),
            )

        def look(table):
            return jnp.take_along_axis(table, low, axis=1)

        def look_up(k):
            return pick(
                [look(tables[k, :, p * LANES : (p + 1) * LANES]) for p in range(PIECES)]
            )

        for plane in range(2):
            base = plane * (2 + 2 * PIECES)
            pos, mom = c_buf[2 * plane, :, where], c_buf[2 * plane + 1, :, where]
            kicked = mom + look_up(2 * plane) + look_up(2 * plane + 1) * pos
            fine_cos, fine_sin = look(phases[base]), look(phases[base + 1])
            coarse_cos = pick([phases[base + 2 + p] for p in range(PIECES)])
            coarse_sin = pick([phases[base + 2 + PIECES + p] for p in range(PIECES)])
            cos = coarse_cos * fine_cos - coarse_sin * fine_sin
            sin = coarse_sin * fine_cos + coarse_cos * fine_sin
            o_buf[2 * plane, :, where] = cos * pos + sin * kicked
            o_buf[2 * plane + 1, :, where] = cos * kicked - sin * pos
        return 0

    each = chunk // LANES
    for step in range(chunks):
        load, load_index, store = moves(step)
        load.wait()
        load_index.wait()
        lax.fori_loop(step * each, (step + 1) * each, track, 0, unroll=unroll)
        store.start()
    for step in range(chunks):
        moves(step)[2].wait()


def on_device(coords, slice_index, fill, others, wake, decay, coef, tunes, chroma):
    _, bunch_dev, part_dev = coords.shape
    n_dom, n_cycle = lax.axis_size("dom"), lax.axis_size("bunch")
    chunk, step_len = 8192, 4096
    chunks = part_dev // chunk
    width = 3 * SLICES + 2 * LANES
    phase_count = 2 * (2 + 2 * PIECES)
    f32 = jnp.float32
    vmem = pl.BlockSpec(memory_space=pltpu.VMEM)
    smem = pl.BlockSpec(memory_space=pltpu.SMEM)
    hbm = pl.BlockSpec(memory_space=pl.ANY)
    dma = pltpu.SemaphoreType.DMA
    tables, phases = pl.pallas_call(
        functools.partial(deposit_kernel, n_cycle, n_dom, chunk, step_len),
        out_shape=(
            jax.ShapeDtypeStruct((4, bunch_dev, SLICES), f32),
            jax.ShapeDtypeStruct((phase_count, 8, LANES), f32),
        ),
        in_specs=[hbm, hbm, vmem, vmem, vmem, smem, smem, smem, smem],
        out_specs=(vmem, vmem),
        scratch_shapes=[
            pltpu.VMEM((bunch_dev, part_dev), f32),
            pltpu.VMEM((bunch_dev, part_dev), f32),
            pltpu.VMEM((bunch_dev, part_dev), jnp.int32),
            pltpu.VMEM((4, BAND, SLICES), f32),
            pltpu.VMEM((bunch_dev, 5 * HIGH, LOW), f32),
            pltpu.VMEM((8, LANES), f32),
            pltpu.VMEM((8, LANES), f32),
            pltpu.VMEM((8, LANES), f32),
            pltpu.VMEM((n_cycle - 1, 8, LANES), f32),
            pltpu.VMEM((bunch_dev, width), f32),
            pltpu.VMEM((n_dom - 1, bunch_dev, width), f32),
            pltpu.VMEM((3, bunch_dev, LANES + SLICES), f32),
            dma((3, chunks)),
            dma((n_cycle - 1,)),
            dma((n_cycle - 1,)),
            dma((n_dom - 1,)),
            dma((n_dom - 1,)),
        ],
        compiler_params=pltpu.CompilerParams(
            collective_id=0, has_side_effects=True, vmem_limit_bytes=40 << 20
        ),
        name="deposit",
    )(coords, slice_index, fill[None], others, wake, decay, coef, tunes, chroma)
    chunk = 4096
    chunks = part_dev // chunk
    return pl.pallas_call(
        functools.partial(track_kernel, chunk, 16),
        out_shape=jax.ShapeDtypeStruct(coords.shape, f32),
        in_specs=[hbm, hbm, vmem, vmem],
        out_specs=hbm,
        scratch_shapes=[
            pltpu.VMEM(coords.shape, f32),
            pltpu.VMEM((bunch_dev, part_dev), jnp.int32),
            pltpu.VMEM(coords.shape, f32),
            dma((2, chunks)),
            dma((chunks,)),
        ],
        compiler_params=pltpu.CompilerParams(vmem_limit_bytes=40 << 20),
        name="track",
    )(coords, slice_index, tables, phases)


def solution(mesh):
    placed = (
        P(None, "bunch", "dom"),
        P("bunch", "dom"),
        P("bunch"),
        P(None, "bunch"),
        P(),
        P(),
        P(),
        P(),
        P(),
    )
    return jax.shard_map(
        on_device, mesh=mesh, in_specs=placed, out_specs=P(None, "bunch", "dom"), check_vma=False
    )
```

time: 736 us -> 41.6 us (0.06)
  matrix products: 453 us -> 0 us
  local copies, waits for them, and re-layouts: 116 us -> 8.78 us
  waiting for transfers between devices: 85.3 us -> 0 us
  other arithmetic: 66.6 us -> 0 us
  Pallas kernels: 0 us -> 32.5 us
  blocking collectives: 10.6 us -> 0 us
    dot_general x19 -> x0, matrix products: 453 us -> none  [the longest x8 279 us: track_block(): jnp.einsum('bcs,bps->bcp', slice_kick, onehot, precision=lax.Precision.HI...]
    ppermute x15 -> x0, waiting for transfers between devices: 85.3 us -> none  [from_behind(): return lax.ppermute(value, axis, pairs)]
    another operation x25 -> x0, other arithmetic: 59.2 us -> none  [the longest x24 59.1 us: track_block(): jnp.stack([cos_x * pos_x + sin_x * mom_xk, cos_x * mom_xk - sin_x * pos_x...]
    slice x27 -> x0, local copies, waits for them, and re-layouts: 53.3 us -> none  [the longest x8 44.2 us: deposit_block(): pos_piece = lax.dynamic_slice_in_dim(coords[0], start, block_len, 1)]
    gather x2 -> x0, local copies, waits for them, and re-layouts: 47.2 us -> none  [slice_tables(): table = shaped[:, :, jnp.broadcast_to(col_ids, (band, band)), offset]]
    pallas_call x0 -> x2, Pallas kernels: none -> 32.5 us  [the longest x1 22.4 us: on_device(): pl.pallas_call(functools.partial(deposit_kernel, n_cycle, n_dom, chunk, s...]
    psum x1 -> x0, blocking collectives: 10.6 us -> none  [on_device(): moments = lax.psum(partial_value, 'dom') * scale_moment]
  transfers between devices with their start and end apart: 15 -> 0, of which waited for: 15 -> 0; matrix products, arithmetic and copies ran while one was open for 0% -> 0% of each run, Pallas kernels for 0% -> 0%
where the time goes in v1:
time: 41.6 us; the launch traced here: 41.3 us
  Pallas kernels  32.5 us (78%)
  local copies, waits for them, and re-layouts  8.78 us (21%)
    pallas_call x1, Pallas kernels, on_device(): pl.pallas_call(functools.partial(deposit_kernel, n_cycle, n_dom, chunk, s...  22.4 us
    pallas_call x1, Pallas kernels, on_device(): pl.pallas_call(functools.partial(track_kernel, chunk, 16), out_shape=jax....  10.1 us
    unnamed x17, local copies, waits for them, and re-layouts  8.78 us

profile of v1, /device:TPU:0, one launch (start us, length us, event | category | flops | bytes accessed | tf_op | source)
XLA Modules:
  0.0 41.3 jit_solution(11827135986853515637)
XLA Ops:
  0.0 1.4 %copy.10.wake = f32[4,512,64]{2,1,0:T(8,128)S(1)} copy(f32[4,512,64]{1,2,0:T(8,128)} %param.13) | data formatting | bytes 1048576 | tf_op args[4]
  1.4 0.0 copy-start
  1.4 2.2 %copy-done = f32[4,8,32768]{2,1,0:T(8,128)S(1)} copy-done((f32[4,8,32768]{2,1,0:T(8,128)S(1)}, f32[4,8,32768]{2,1,0:T(8,128)}, u32[]{:S(2)}) %copy-start) | copy-done | bytes 4194328
  3.6 0.0 copy-start.1
  3.6 1.2 %copy-done.1 = s32[8,32768]{1,0:T(8,128)S(1)} copy-done((s32[8,32768]{1,0:T(8,128)S(1)}, s32[8,32768]{1,0:T(8,128)}, u32[]{:S(2)}) %copy-start.1) | copy-done | bytes 1048600
  4.8 0.0 copy-start.2
  4.8 0.7 %copy-done.2 = f32[2,112]{1,0:T(2,128)S(1)} copy-done((f32[2,112]{1,0:T(2,128)S(1)}, f32[2,112]{1,0:T(2,128)}, u32[]{:S(2)}) %copy-start.2) | copy-done | bytes 920
  5.5 0.0 copy-start.3
  5.5 0.7 %copy-done.3 = f32[2,8]{1,0:T(2,128)S(1)} copy-done((f32[2,8]{1,0:T(2,128)S(1)}, f32[2,8]{1,0:T(2,128)}, u32[]{:S(2)}) %copy-start.3) | copy-done | bytes 88
  6.2 0.0 copy-start.4
  6.2 0.7 %copy-done.4 = f32[2,8]{1,0:T(2,128)S(1)} copy-done((f32[2,8]{1,0:T(2,128)S(1)}, f32[2,8]{1,0:T(2,128)}, u32[]{:S(2)}) %copy-start.4) | copy-done | bytes 88
  6.8 0.0 copy-start.5
  6.8 0.7 %copy-done.5 = s32[112]{0:T(128)S(1)} copy-done((s32[112]{0:T(128)S(1)}, s32[112]{0:T(128)}, u32[]{:S(2)}) %copy-start.5) | copy-done | bytes 472
  7.5 0.0 copy-start.6
  7.5 0.7 %copy-done.6 = f32[2]{0:T(128)S(1)} copy-done((f32[2]{0:T(128)S(1)}, f32[2]{0:T(128)}, u32[]{:S(2)}) %copy-start.6) | copy-done | bytes 32
  8.1 0.0 copy-start.7
  8.1 0.7 %copy-done.7 = f32[2]{0:T(128)S(1)} copy-done((f32[2]{0:T(128)S(1)}, f32[2]{0:T(128)}, u32[]{:S(2)}) %copy-start.7) | copy-done | bytes 32
  8.8 22.4 %deposit.1 = (f32[4,8,512]{2,1,0:T(8,128)S(1)}, f32[20,8,128]{2,1,0:T(8,128)S(1)}) custom-call(f32[4,8,32768]{2,1,0:T(8,128)S(1)} %copy-done, s32[8,32768]{1,0:T(8,128)S(1)} %copy-done.1, s32[1,112]{1,0:T(1,128)S(1)} %bitcast.1, f32[2,112]{1,0:T(2,128)S(1)} %copy-done.2, f32[4,512,64]{2,1,0:T(8,128)S(1)} %copy.10.wake, f32[2,8]{1,0:T(2,128)S(1)} %copy-done.3, ...), custom_call_target="tpu_custom_call" | custom-call | tf_op jit(solution)/shard_map/deposit/pallas_call | solution.py:356
  31.2 10.1 %track.1 = f32[4,8,32768]{2,1,0:T(8,128)} custom-call(f32[4,8,32768]{2,1,0:T(8,128)S(1)} %copy-done, s32[8,32768]{1,0:T(8,128)S(1)} %copy-done.1, f32[4,8,512]{2,1,0:T(8,128)S(1)} %get-tuple-element.7.tables, f32[20,8,128]{2,1,0:T(8,128)S(1)} %get-tuple-element.8.phases), custom_call_target="tpu_custom_call" | custom-call | tf_op jit(solution)/shard_map/track/pallas_call | solution.py:390
Async XLA Ops:
  1.4 2.2 %copy-start = (f32[4,8,32768]{2,1,0:T(8,128)S(1)}, f32[4,8,32768]{2,1,0:T(8,128)}, u32[]{:S(2)}) copy-start(f32[4,8,32768]{2,1,0:T(8,128)} %coords.3) | copy-start | bytes 12582916
  3.6 1.2 %copy-start.1 = (s32[8,32768]{1,0:T(8,128)S(1)}, s32[8,32768]{1,0:T(8,128)}, u32[]{:S(2)}) copy-start(s32[8,32768]{1,0:T(8,128)} %index.3) | copy-start | bytes 3145732
  4.8 0.7 %copy-start.2 = (f32[2,112]{1,0:T(2,128)S(1)}, f32[2,112]{1,0:T(2,128)}, u32[]{:S(2)}) copy-start(f32[2,112]{1,0:T(2,128)} %others.1) | copy-start | bytes 2692
  5.5 0.7 %copy-start.3 = (f32[2,8]{1,0:T(2,128)S(1)}, f32[2,8]{1,0:T(2,128)}, u32[]{:S(2)}) copy-start(f32[2,8]{1,0:T(2,128)} %decay.1) | copy-start | bytes 196
  6.2 0.7 %copy-start.4 = (f32[2,8]{1,0:T(2,128)S(1)}, f32[2,8]{1,0:T(2,128)}, u32[]{:S(2)}) copy-start(f32[2,8]{1,0:T(2,128)} %coef.1) | copy-start | bytes 196
  6.8 0.7 %copy-start.5 = (s32[112]{0:T(128)S(1)}, s32[112]{0:T(128)}, u32[]{:S(2)}) copy-start(s32[112]{0:T(128)} %param.11) | copy-start | bytes 1348
  7.5 0.7 %copy-start.6 = (f32[2]{0:T(128)S(1)}, f32[2]{0:T(128)}, u32[]{:S(2)}) copy-start(f32[2]{0:T(128)} %tunes.1) | copy-start | bytes 28
  8.1 0.7 %copy-start.7 = (f32[2]{0:T(128)S(1)}, f32[2]{0:T(128)}, u32[]{:S(2)}) copy-start(f32[2]{0:T(128)} %chroma.1) | copy-start | bytes 28

commit v2 on v1

--- a/solution.py
+++ b/solution.py
@@ -41,10 +41,15 @@
     chroma,
     tables,
     phases,
-    x_buf,
-    y_buf,
+    c_buf,
     i_buf,
+    fill_v,
+    others_v,
     wake_t,
+    decay_v,
+    coef_v,
+    tunes_v,
+    chroma_v,
     grid_sum,
     slots,
     outgoing,
@@ -54,27 +59,51 @@
     theirs,
     padded,
     in_sem,
+    small_sem,
     block_send,
     block_recv,
     dom_send,
     dom_recv,
 ):
-    bunch_dev, part_dev = x_buf.shape
+    bunch_dev, part_dev = i_buf.shape
     slot_dev = fill.shape[1]
     chunks = part_dev // chunk
     me_b, me_d = lax.axis_index("bunch"), lax.axis_index("dom")
 
-    def loads(step):
+    small = [
+        pltpu.make_async_copy(source, target, small_sem.at[k])
+        for k, (source, target) in enumerate(
+            (
+                (tunes, tunes_v),
+                (chroma, chroma_v),
+                (decay, decay_v),
+                (coef, coef_v),
+                (fill, fill_v),
+                (others, others_v),
+                (wake, wake_t),
+            )
+        )
+    ]
+
+    def load(plane, step):
         where = pl.ds(pl.multiple_of(step * chunk, chunk), chunk)
-        return (
-            pltpu.make_async_copy(coords.at[0, :, where], x_buf.at[:, where], in_sem.at[0, step]),
-            pltpu.make_async_copy(coords.at[2, :, where], y_buf.at[:, where], in_sem.at[1, step]),
-            pltpu.make_async_copy(index.at[:, where], i_buf.at[:, where], in_sem.at[2, step]),
-        )
-
-    for plane in range(3):
+        if plane == 4:
+            return pltpu.make_async_copy(
+                index.at[:, where], i_buf.at[:, where], in_sem.at[4, step]
+            )
+        return pltpu.make_async_copy(
+            coords.at[plane, :, where], c_buf.at[plane, :, where], in_sem.at[plane, step]
+        )
+
+    for copy in small[:-1]:
+        copy.start()
+    for step in range(chunks):
+        load(0, step).start()
+        load(2, step).start()
+    for plane in (4, 1, 3):
         for step in range(chunks):
-            loads(step)[plane].start()
+            load(plane, step).start()
+    small[-1].start()
 
     cycle_peers = [(lax.rem(me_b + k, n_cycle), me_d) for k in range(1, n_cycle)]
     dom_peers = [(me_b, lax.rem(me_d + k, n_dom)) for k in range(1, n_dom)]
@@ -89,15 +118,20 @@
     half_f = half.astype(jnp.float32)
     zeros = jnp.zeros((8, LANES), jnp.float32)
 
-    def by_row(ref, plane):
-        built = zeros
-        for term in range(8):
-            built = jnp.where(row == term, ref[plane, term], built)
-        return built
-
-    decay_x, decay_y = by_row(decay, 0), by_row(decay, 1)
+    for copy in small[:-1]:
+        copy.wait()
+    slots[...] = jnp.zeros_like(slots)
+    slots[0:2, 0:slot_dev] = others_v[...]
+    slots[2:3, 0:slot_dev] = fill_v[...].astype(jnp.float32)
+    slots[3:5, 0:8] = decay_v[...]
+    slots[5:7, 0:8] = coef_v[...]
+
+    def by_row(at):
+        return lanes_sum(jnp.where(lane == row, slots[at : at + 1, :], 0.0))
+
+    decay_x, decay_y = by_row(3), by_row(4)
     decay_both = jnp.where(second, decay_y, decay_x)
-    coef_both = jnp.where(second, by_row(coef, 1), by_row(coef, 0))
+    coef_both = jnp.where(second, by_row(6), by_row(5))
     back = (slot_dev - 1 - lane).astype(jnp.float32)
     inside = lane < slot_dev
     back = jnp.where(inside, back, 0.0)
@@ -108,8 +142,8 @@
     ahead = coef_both * jnp.exp(-decay_both * half_f)
 
     lower = row < 4
-    chroma_rows = jnp.where(lower, chroma[0], chroma[1])
-    tune_rows = jnp.where(lower, tunes[0], tunes[1])
+    chroma_rows = jnp.where(lower, chroma_v[:, 0:1], chroma_v[:, 1:2])
+    tune_rows = jnp.where(lower, tunes_v[:, 0:1], tunes_v[:, 1:2])
     fine = chroma_rows * (lane.astype(jnp.float32) * (2.0 / SLICES))
     first = 2.0 * ((lane & 3).astype(jnp.float32) * LANES + 0.5) / SLICES - 1.0
     coarse = 2.0 * math.pi * tune_rows + chroma_rows * first
@@ -125,22 +159,16 @@
             phases[base + 2 + piece] = jnp.broadcast_to(coarse_cos[spot], (8, LANES))
             phases[base + 2 + PIECES + piece] = jnp.broadcast_to(coarse_sin[spot], (8, LANES))
 
-    for plane in range(4):
-        wake_t[plane] = jnp.transpose(wake[plane])
-    slots[...] = jnp.zeros_like(slots)
-    slots[0:2, 0:slot_dev] = others[...]
-    slots[2:3, 0:slot_dev] = fill[...].astype(jnp.float32)
-
     def add_up(step, total):
-        for plane in range(2):
-            loads(step)[plane].wait()
+        load(0, step).wait()
+        load(2, step).wait()
         at = pl.multiple_of(step * chunk, chunk)
         sums = list(total)
         for piece in range(chunk // LANES):
             where = pl.ds(at + piece * LANES, LANES)
             k = piece % 4
-            sums[k] = sums[k] + x_buf[:, where]
-            sums[4 + k] = sums[4 + k] + y_buf[:, where]
+            sums[k] = sums[k] + c_buf[0, :, where]
+            sums[4 + k] = sums[4 + k] + c_buf[2, :, where]
         return tuple(sums)
 
     sums = lax.fori_loop(0, chunks, add_up, (zeros,) * 8)
@@ -183,7 +211,7 @@
     def deposit(step, _):
         at = pl.multiple_of(step * step_len, step_len)
         where = pl.ds(at, step_len)
-        x, y, level = x_buf[:, where], y_buf[:, where], i_buf[:, where]
+        x, y, level = c_buf[0, :, where], c_buf[2, :, where], i_buf[:, where]
         x_low = x - x.astype(jnp.bfloat16).astype(jnp.float32)
         y_low = y - y.astype(jnp.bfloat16).astype(jnp.float32)
         high = lax.shift_right_logical(level, shift)
@@ -202,7 +230,7 @@
         return 0
 
     for step in range(chunks):
-        loads(step)[2].wait()
+        load(4, step).wait()
     lax.fori_loop(0, part_dev // step_len, deposit, 0)
 
     for b in range(bunch_dev):
@@ -253,6 +281,10 @@
         dom_copy(k).wait()
         total = total + theirs[k]
 
+    small[-1].wait()
+    for plane in (1, 3):
+        for step in range(chunks):
+            load(plane, step).wait()
     scale_moment = SLICES / (part_dev * n_dom)
     for v in range(3):
         padded[v, :, 0:LANES] = zeros
@@ -272,28 +304,15 @@
     tables[3] = kicks[3]
 
 
-def track_kernel(
-    chunk, unroll, coords, index, tables, phases, result, c_buf, i_buf, o_buf, in_sem, out_sem
-):
+def track_kernel(chunk, unroll, c_buf, i_buf, tables, phases, result, o_buf, out_sem):
     part_dev = i_buf.shape[1]
     chunks = part_dev // chunk
 
-    def moves(step):
+    def store(step):
         where = pl.ds(step * chunk, chunk)
-        return (
-            pltpu.make_async_copy(
-                coords.at[:, :, where], c_buf.at[:, :, where], in_sem.at[0, step]
-            ),
-            pltpu.make_async_copy(index.at[:, where], i_buf.at[:, where], in_sem.at[1, step]),
-            pltpu.make_async_copy(
-                o_buf.at[:, :, where], result.at[:, :, where], out_sem.at[step]
-            ),
-        )
-
-    for step in range(chunks):
-        load, load_index, _ = moves(step)
-        load.start()
-        load_index.start()
+        return pltpu.make_async_copy(
+            o_buf.at[:, :, where], result.at[:, :, where], out_sem.at[step]
+        )
 
     def track(step, _):
         where = pl.ds(pl.multiple_of(step * LANES, LANES), LANES)
@@ -332,40 +351,42 @@
 
     each = chunk // LANES
     for step in range(chunks):
-        load, load_index, store = moves(step)
-        load.wait()
-        load_index.wait()
         lax.fori_loop(step * each, (step + 1) * each, track, 0, unroll=unroll)
-        store.start()
+        store(step).start()
     for step in range(chunks):
-        moves(step)[2].wait()
+        store(step).wait()
 
 
 def on_device(coords, slice_index, fill, others, wake, decay, coef, tunes, chroma):
+    hold = lambda a: pltpu.with_memory_space_constraint(a, pltpu.HBM)
     _, bunch_dev, part_dev = coords.shape
     n_dom, n_cycle = lax.axis_size("dom"), lax.axis_size("bunch")
-    chunk, step_len = 8192, 4096
+    chunk, step_len = 8192, 8192
     chunks = part_dev // chunk
     width = 3 * SLICES + 2 * LANES
     phase_count = 2 * (2 + 2 * PIECES)
     f32 = jnp.float32
     vmem = pl.BlockSpec(memory_space=pltpu.VMEM)
-    smem = pl.BlockSpec(memory_space=pltpu.SMEM)
-    hbm = pl.BlockSpec(memory_space=pl.ANY)
+    hbm = pl.BlockSpec(memory_space=pltpu.HBM)
     dma = pltpu.SemaphoreType.DMA
-    tables, phases = pl.pallas_call(
+    tables, phases, held, held_index = pl.pallas_call(
         functools.partial(deposit_kernel, n_cycle, n_dom, chunk, step_len),
         out_shape=(
             jax.ShapeDtypeStruct((4, bunch_dev, SLICES), f32),
             jax.ShapeDtypeStruct((phase_count, 8, LANES), f32),
+            jax.ShapeDtypeStruct(coords.shape, f32),
+            jax.ShapeDtypeStruct((bunch_dev, part_dev), jnp.int32),
         ),
-        in_specs=[hbm, hbm, vmem, vmem, vmem, smem, smem, smem, smem],
-        out_specs=(vmem, vmem),
+        in_specs=[hbm] * 9,
+        out_specs=(vmem,) * 4,
         scratch_shapes=[
-            pltpu.VMEM((bunch_dev, part_dev), f32),
-            pltpu.VMEM((bunch_dev, part_dev), f32),
-            pltpu.VMEM((bunch_dev, part_dev), jnp.int32),
+            pltpu.VMEM((1, fill.shape[0]), jnp.int32),
+            pltpu.VMEM(others.shape, f32),
             pltpu.VMEM((4, BAND, SLICES), f32),
+            pltpu.VMEM(decay.shape, f32),
+            pltpu.VMEM(coef.shape, f32),
+            pltpu.VMEM((1, 2), f32),
+            pltpu.VMEM((1, 2), f32),
             pltpu.VMEM((bunch_dev, 5 * HIGH, LOW), f32),
             pltpu.VMEM((8, LANES), f32),
             pltpu.VMEM((8, LANES), f32),
@@ -374,7 +395,8 @@
             pltpu.VMEM((bunch_dev, width), f32),
             pltpu.VMEM((n_dom - 1, bunch_dev, width), f32),
             pltpu.VMEM((3, bunch_dev, LANES + SLICES), f32),
-            dma((3, chunks)),
+            dma((5, chunks)),
+            dma((7,)),
             dma((n_cycle - 1,)),
             dma((n_cycle - 1,)),
             dma((n_dom - 1,)),
@@ -384,24 +406,33 @@
             collective_id=0, has_side_effects=True, vmem_limit_bytes=40 << 20
         ),
         name="deposit",
-    )(coords, slice_index, fill[None], others, wake, decay, coef, tunes, chroma)
+    )(
+        *(
+            hold(a)
+            for a in (
+                coords,
+                slice_index,
+                fill[None],
+                others,
+                jnp.swapaxes(wake, 1, 2),
+                decay,
+                coef,
+                tunes[None],
+                chroma[None],
+            )
+        )
+    )
     chunk = 4096
     chunks = part_dev // chunk
     return pl.pallas_call(
         functools.partial(track_kernel, chunk, 16),
         out_shape=jax.ShapeDtypeStruct(coords.shape, f32),
-        in_specs=[hbm, hbm, vmem, vmem],
+        in_specs=[vmem] * 4,
         out_specs=hbm,
-        scratch_shapes=[
-            pltpu.VMEM(coords.shape, f32),
-            pltpu.VMEM((bunch_dev, part_dev), jnp.int32),
-            pltpu.VMEM(coords.shape, f32),
-            dma((2, chunks)),
-            dma((chunks,)),
-        ],
+        scratch_shapes=[pltpu.VMEM(coords.shape, f32), dma((chunks,))],
         compiler_params=pltpu.CompilerParams(vmem_limit_bytes=40 << 20),
         name="track",
-    )(coords, slice_index, tables, phases)
+    )(held, held_index, tables, phases)
 
 
 def solution(mesh):

time: 41.6 us -> 29.6 us (0.71)
  local copies, waits for them, and re-layouts: 8.78 us -> 0 us
  Pallas kernels: 32.5 us -> 29.5 us
    unnamed x17 -> x0, local copies, waits for them, and re-layouts: 8.78 us -> none
    pallas_call x1, Pallas kernels: 10.1 us -> 8.26 us  [on_device(): pl.pallas_call(functools.partial(track_kernel, chunk, 16), out_shape=jax....]
    pallas_call x1, Pallas kernels: 22.4 us -> 21.2 us  [on_device(): pl.pallas_call(functools.partial(deposit_kernel, n_cycle, n_dom, chunk, s...]
where the time goes in v2:
time: 29.6 us; the launch traced here: 29.5 us
  Pallas kernels  29.5 us (100%)
    pallas_call x1, Pallas kernels, on_device(): pl.pallas_call(functools.partial(deposit_kernel, n_cycle, n_dom, chunk, s...  21.2 us
    pallas_call x1, Pallas kernels, on_device(): pl.pallas_call(functools.partial(track_kernel, chunk, 16), out_shape=jax....  8.26 us

profile of v2, /device:TPU:0, one launch (start us, length us, event | category | flops | bytes accessed | tf_op | source)
XLA Modules:
  0.0 29.5 jit_solution(779215839157274975)
XLA Ops:
  0.0 21.2 %deposit.1 = (f32[4,8,512]{2,1,0:T(8,128)S(1)}, f32[20,8,128]{2,1,0:T(8,128)S(1)}, f32[4,8,32768]{2,1,0:T(8,128)S(1)}, s32[8,32768]{1,0:T(8,128)S(1)}) custom-call(f32[4,8,32768]{2,1,0:T(8,128)} %coords.1, s32[8,32768]{1,0:T(8,128)} %index.1, s32[1,112]{1,0:T(1,128)} %bitcast.5, f32[2,112]{1,0:T(2,128)} %others.1, f32[4,64,512]{2,1,0:T(8,128)} %bitcast.4, ...), custom_call_target="tpu_custom_call" | custom-call | tf_op jit(solution)/shard_map/deposit/pallas_call | solution.py:372
  21.2 8.3 %track.1 = f32[4,8,32768]{2,1,0:T(8,128)} custom-call(f32[4,8,32768]{2,1,0:T(8,128)S(1)} %get-tuple-element.9.c_buf, s32[8,32768]{1,0:T(8,128)S(1)} %get-tuple-element.10.i_buf, f32[4,8,512]{2,1,0:T(8,128)S(1)} %get-tuple-element.11.tables, f32[20,8,128]{2,1,0:T(8,128)S(1)} %get-tuple-element.12.phases), custom_call_target="tpu_custom_call" | custom-call | tf_op jit(solution)/shard_map/track/pallas_call | solution.py:427

commit v3 on v2

--- a/solution.py
+++ b/solution.py
@@ -100,7 +100,8 @@
     for step in range(chunks):
         load(0, step).start()
         load(2, step).start()
-    for plane in (4, 1, 3):
+        load(4, step).start()
+    for plane in (1, 3):
         for step in range(chunks):
             load(plane, step).start()
     small[-1].start()
@@ -158,49 +159,6 @@
             spot = (slice(at, at + 1), slice(piece, piece + 1))
             phases[base + 2 + piece] = jnp.broadcast_to(coarse_cos[spot], (8, LANES))
             phases[base + 2 + PIECES + piece] = jnp.broadcast_to(coarse_sin[spot], (8, LANES))
-
-    def add_up(step, total):
-        load(0, step).wait()
-        load(2, step).wait()
-        at = pl.multiple_of(step * chunk, chunk)
-        sums = list(total)
-        for piece in range(chunk // LANES):
-            where = pl.ds(at + piece * LANES, LANES)
-            k = piece % 4
-            sums[k] = sums[k] + c_buf[0, :, where]
-            sums[4 + k] = sums[4 + k] + c_buf[2, :, where]
-        return tuple(sums)
-
-    sums = lax.fori_loop(0, chunks, add_up, (zeros,) * 8)
-    sum_x = lanes_sum((sums[0] + sums[1]) + (sums[2] + sums[3]))
-    sum_y = lanes_sum((sums[4] + sums[5]) + (sums[6] + sums[7]))
-    mean = 1.0 / (part_dev * n_dom)
-    diagonal = lane == row
-    once = jnp.where(me_d == 0, 1.0, 0.0)
-    filled = slots[2:3, :]
-    tracked = lane[0:1] < bunch_dev
-    track_x = rows_sum(jnp.where(diagonal, sum_x, 0.0)) * mean
-    track_y = rows_sum(jnp.where(diagonal, sum_y, 0.0)) * mean
-    centre_x = filled * jnp.where(tracked, track_x, slots[0:1, :] * once)
-    centre_y = filled * jnp.where(tracked, track_y, slots[1:2, :] * once)
-    block_own[...] = jnp.where(
-        second, lanes_sum(tail_y * centre_y), lanes_sum(tail_x * centre_x)
-    )
-
-    pl.semaphore_wait(barrier, n_cycle - 1 + n_dom - 1)
-
-    def block_copy(k):
-        return pltpu.make_async_remote_copy(
-            src_ref=block_own,
-            dst_ref=block_got.at[k],
-            send_sem=block_send.at[k],
-            recv_sem=block_recv.at[k],
-            device_id=cycle_peers[k],
-            device_id_type=MESH,
-        )
-
-    for k in range(n_cycle - 1):
-        block_copy(k).start()
 
     grid_sum[...] = jnp.zeros_like(grid_sum)
     high_ids = lax.broadcasted_iota(jnp.int32, (HIGH, step_len), 0)
@@ -229,9 +187,58 @@
             )
         return 0
 
-    for step in range(chunks):
+    for plane in (0, 2, 4):
+        load(plane, 0).wait()
+    lax.fori_loop(0, chunk // step_len, deposit, 0)
+
+    for step in range(1, chunks):
+        load(0, step).wait()
+        load(2, step).wait()
+
+    def add_up(step, total):
+        at = pl.multiple_of(step * chunk, chunk)
+        sums = list(total)
+        for piece in range(chunk // LANES):
+            where = pl.ds(at + piece * LANES, LANES)
+            k = piece % 4
+            sums[k] = sums[k] + c_buf[0, :, where]
+            sums[4 + k] = sums[4 + k] + c_buf[2, :, where]
+        return tuple(sums)
+
+    sums = lax.fori_loop(0, chunks, add_up, (zeros,) * 8)
+    sum_x = lanes_sum((sums[0] + sums[1]) + (sums[2] + sums[3]))
+    sum_y = lanes_sum((sums[4] + sums[5]) + (sums[6] + sums[7]))
+    mean = 1.0 / (part_dev * n_dom)
+    diagonal = lane == row
+    once = jnp.where(me_d == 0, 1.0, 0.0)
+    filled = slots[2:3, :]
+    tracked = lane[0:1] < bunch_dev
+    track_x = rows_sum(jnp.where(diagonal, sum_x, 0.0)) * mean
+    track_y = rows_sum(jnp.where(diagonal, sum_y, 0.0)) * mean
+    centre_x = filled * jnp.where(tracked, track_x, slots[0:1, :] * once)
+    centre_y = filled * jnp.where(tracked, track_y, slots[1:2, :] * once)
+    block_own[...] = jnp.where(
+        second, lanes_sum(tail_y * centre_y), lanes_sum(tail_x * centre_x)
+    )
+
+    pl.semaphore_wait(barrier, n_cycle - 1 + n_dom - 1)
+
+    def block_copy(k):
+        return pltpu.make_async_remote_copy(
+            src_ref=block_own,
+            dst_ref=block_got.at[k],
+            send_sem=block_send.at[k],
+            recv_sem=block_recv.at[k],
+            device_id=cycle_peers[k],
+            device_id_type=MESH,
+        )
+
+    for k in range(n_cycle - 1):
+        block_copy(k).start()
+
+    for step in range(1, chunks):
         load(4, step).wait()
-    lax.fori_loop(0, part_dev // step_len, deposit, 0)
+    lax.fori_loop(chunk // step_len, part_dev // step_len, deposit, 0)
 
     for b in range(bunch_dev):
         part = grid_sum[b]
@@ -309,7 +316,7 @@
     chunks = part_dev // chunk
 
     def store(step):
-        where = pl.ds(step * chunk, chunk)
+        where = pl.ds(pl.multiple_of(step * chunk, chunk), chunk)
         return pltpu.make_async_copy(
             o_buf.at[:, :, where], result.at[:, :, where], out_sem.at[step]
         )
@@ -350,9 +357,12 @@
         return 0
 
     each = chunk // LANES
-    for step in range(chunks):
-        lax.fori_loop(step * each, (step + 1) * each, track, 0, unroll=unroll)
+    def run(step, _):
+        lax.fori_loop(0, each, lambda k, z: track(step * each + k, z), 0, unroll=unroll)
         store(step).start()
+        return 0
+
+    lax.fori_loop(0, chunks, run, 0)
     for step in range(chunks):
         store(step).wait()
 
@@ -425,7 +435,7 @@
     chunk = 4096
     chunks = part_dev // chunk
     return pl.pallas_call(
-        functools.partial(track_kernel, chunk, 16),
+        functools.partial(track_kernel, chunk, 32),
         out_shape=jax.ShapeDtypeStruct(coords.shape, f32),
         in_specs=[vmem] * 4,
         out_specs=hbm,

time: 29.6 us -> 27.3 us (0.922)
  Pallas kernels: 29.5 us -> 27.2 us
    pallas_call x1, Pallas kernels: 21.2 us -> 19.5 us  [on_device(): pl.pallas_call(functools.partial(deposit_kernel, n_cycle, n_dom, chunk, s...]
    pallas_call x1, Pallas kernels: 8.26 us -> 7.7 us  [on_device(): pl.pallas_call(functools.partial(track_kernel, chunk, 32), out_shape=jax....]
where the time goes in v3:
time: 27.3 us; the launch traced here: 27.2 us
  Pallas kernels  27.2 us (100%)
    pallas_call x1, Pallas kernels, on_device(): pl.pallas_call(functools.partial(deposit_kernel, n_cycle, n_dom, chunk, s...  19.5 us
    pallas_call x1, Pallas kernels, on_device(): pl.pallas_call(functools.partial(track_kernel, chunk, 32), out_shape=jax....  7.7 us

profile of v3, /device:TPU:0, one launch (start us, length us, event | category | flops | bytes accessed | tf_op | source)
XLA Modules:
  0.0 27.2 jit_solution(14675229769988004611)
XLA Ops:
  0.0 19.5 %deposit.1 = (f32[4,8,512]{2,1,0:T(8,128)S(1)}, f32[20,8,128]{2,1,0:T(8,128)S(1)}, f32[4,8,32768]{2,1,0:T(8,128)S(1)}, s32[8,32768]{1,0:T(8,128)S(1)}) custom-call(f32[4,8,32768]{2,1,0:T(8,128)} %coords.1, s32[8,32768]{1,0:T(8,128)} %index.1, s32[1,112]{1,0:T(1,128)} %bitcast.5, f32[2,112]{1,0:T(2,128)} %others.1, f32[4,64,512]{2,1,0:T(8,128)} %bitcast.4, ...), custom_call_target="tpu_custom_call" | custom-call | tf_op jit(solution)/shard_map/deposit/pallas_call | solution.py:382
  19.5 7.7 %track.1 = f32[4,8,32768]{2,1,0:T(8,128)} custom-call(f32[4,8,32768]{2,1,0:T(8,128)S(1)} %get-tuple-element.9.c_buf, s32[8,32768]{1,0:T(8,128)S(1)} %get-tuple-element.10.i_buf, f32[4,8,512]{2,1,0:T(8,128)S(1)} %get-tuple-element.11.tables, f32[20,8,128]{2,1,0:T(8,128)S(1)} %get-tuple-element.12.phases), custom_call_target="tpu_custom_call" | custom-call | tf_op jit(solution)/shard_map/track/pallas_call | solution.py:437

commit v4 on v3

--- a/solution.py
+++ b/solution.py
@@ -57,6 +57,8 @@
     block_got,
     mine,
     theirs,
+    long_mine,
+    long_theirs,
     padded,
     in_sem,
     small_sem,
@@ -252,6 +254,19 @@
                 at = v * SLICES + h * LOW
                 mine[b : b + 1, at : at + LOW] = kinds[v][h : h + 1]
 
+    def dom_copy(source, target, kind, k):
+        return pltpu.make_async_remote_copy(
+            src_ref=source,
+            dst_ref=target.at[k],
+            send_sem=dom_send.at[kind, k],
+            recv_sem=dom_recv.at[kind, k],
+            device_id=dom_peers[k],
+            device_id_type=MESH,
+        )
+
+    for k in range(n_dom - 1):
+        dom_copy(mine, theirs, 0, k).start()
+
     carried = block_own[...]
     for k in reversed(range(n_cycle - 1)):
         block_copy(k).wait()
@@ -263,29 +278,18 @@
         inner = coef_both * jnp.exp(-decay_both * gap) * centre
         pieces = pieces + jnp.where(half > j, inner, 0.0)
     long_row = rows_sum(pieces)
-    long_at = 3 * SLICES
-    mine[:, long_at : long_at + LANES] = jnp.broadcast_to(
+    long_mine[:, 0:LANES] = jnp.broadcast_to(
         lanes_sum(jnp.where(lane == row, long_row, 0.0)), (8, LANES)
     )
-    mine[:, long_at + LANES : long_at + 2 * LANES] = jnp.broadcast_to(
+    long_mine[:, LANES : 2 * LANES] = jnp.broadcast_to(
         lanes_sum(jnp.where(lane == row + 64, long_row, 0.0)), (8, LANES)
     )
 
-    def dom_copy(k):
-        return pltpu.make_async_remote_copy(
-            src_ref=mine,
-            dst_ref=theirs.at[k],
-            send_sem=dom_send.at[k],
-            recv_sem=dom_recv.at[k],
-            device_id=dom_peers[k],
-            device_id_type=MESH,
-        )
-
     for k in range(n_dom - 1):
-        dom_copy(k).start()
+        dom_copy(long_mine, long_theirs, 1, k).start()
     total = mine[...]
     for k in range(n_dom - 1):
-        dom_copy(k).wait()
+        dom_copy(mine, theirs, 0, k).wait()
         total = total + theirs[k]
 
     small[-1].wait()
@@ -303,8 +307,11 @@
         )
         for c, source in enumerate((mom_x, count, mom_y, count)):
             kicks[c] = kicks[c] + wake_t[c, lag : lag + 1, :] * source
-    long_x = total[:, long_at : long_at + 1]
-    long_y = total[:, long_at + LANES : long_at + LANES + 1]
+    long_total = long_mine[...]
+    for k in range(n_dom - 1):
+        dom_copy(long_mine, long_theirs, 1, k).wait()
+        long_total = long_total + long_theirs[k]
+    long_x, long_y = long_total[:, 0:1], long_total[:, LANES : LANES + 1]
     tables[0] = kicks[0] + long_x
     tables[1] = kicks[1]
     tables[2] = kicks[2] + long_y
@@ -373,7 +380,7 @@
     n_dom, n_cycle = lax.axis_size("dom"), lax.axis_size("bunch")
     chunk, step_len = 8192, 8192
     chunks = part_dev // chunk
-    width = 3 * SLICES + 2 * LANES
+    width = 3 * SLICES
     phase_count = 2 * (2 + 2 * PIECES)
     f32 = jnp.float32
     vmem = pl.BlockSpec(memory_space=pltpu.VMEM)
@@ -404,13 +411,15 @@
             pltpu.VMEM((n_cycle - 1, 8, LANES), f32),
             pltpu.VMEM((bunch_dev, width), f32),
             pltpu.VMEM((n_dom - 1, bunch_dev, width), f32),
+            pltpu.VMEM((bunch_dev, 2 * LANES), f32),
+            pltpu.VMEM((n_dom - 1, bunch_dev, 2 * LANES), f32),
             pltpu.VMEM((3, bunch_dev, LANES + SLICES), f32),
             dma((5, chunks)),
             dma((7,)),
             dma((n_cycle - 1,)),
             dma((n_cycle - 1,)),
-            dma((n_dom - 1,)),
-            dma((n_dom - 1,)),
+            dma((2, n_dom - 1)),
+            dma((2, n_dom - 1)),
         ],
         compiler_params=pltpu.CompilerParams(
             collective_id=0, has_side_effects=True, vmem_limit_bytes=40 << 20

time: 27.3 us -> 27.1 us (level)
  Pallas kernels: 27.2 us -> 26.9 us
where the time goes in v4:
time: 27.1 us; the launch traced here: 26.9 us
  Pallas kernels  26.9 us (99%)
    pallas_call x1, Pallas kernels, on_device(): pl.pallas_call(functools.partial(deposit_kernel, n_cycle, n_dom, chunk, s...  19.2 us
    pallas_call x1, Pallas kernels, on_device(): pl.pallas_call(functools.partial(track_kernel, chunk, 32), out_shape=jax....  7.7 us

profile of v4, /device:TPU:0, one launch (start us, length us, event | category | flops | bytes accessed | tf_op | source)
XLA Modules:
  0.0 26.9 jit_solution(1503824433636895624)
XLA Ops:
  0.0 19.2 %deposit.1 = (f32[4,8,512]{2,1,0:T(8,128)S(1)}, f32[20,8,128]{2,1,0:T(8,128)S(1)}, f32[4,8,32768]{2,1,0:T(8,128)S(1)}, s32[8,32768]{1,0:T(8,128)S(1)}) custom-call(f32[4,8,32768]{2,1,0:T(8,128)} %coords.1, s32[8,32768]{1,0:T(8,128)} %index.1, s32[1,112]{1,0:T(1,128)} %bitcast.5, f32[2,112]{1,0:T(2,128)} %others.1, f32[4,64,512]{2,1,0:T(8,128)} %bitcast.4, ...), custom_call_target="tpu_custom_call" | custom-call | tf_op jit(solution)/shard_map/deposit/pallas_call | solution.py:389
  19.2 7.7 %track.1 = f32[4,8,32768]{2,1,0:T(8,128)} custom-call(f32[4,8,32768]{2,1,0:T(8,128)S(1)} %get-tuple-element.9.c_buf, s32[8,32768]{1,0:T(8,128)S(1)} %get-tuple-element.10.i_buf, f32[4,8,512]{2,1,0:T(8,128)S(1)} %get-tuple-element.11.tables, f32[20,8,128]{2,1,0:T(8,128)S(1)} %get-tuple-element.12.phases), custom_call_target="tpu_custom_call" | custom-call | tf_op jit(solution)/shard_map/track/pallas_call | solution.py:446
